TPU v7x, 32 devices: a whole 2x2x4 slice. The times are simulated.
32 devices in a mesh: groups: 2 (over y), context: 4 (over z), tensor: 4 (over x, core).
Axes of the slice: x: 2, y: 2, z: 4, core: 2. Of those that a mesh axis runs over, the one named last changes fastest.
Arguments:
- inputs: bfloat16 [4096, 1024], P(('groups', 'context')), parts along dimension 0, may hold values from -6 to 6
- frame_valid: int32 [4096], P(('groups', 'context')), parts along dimension 0, may hold values from 0 to 1, as said below
- norm1_gain: float32 [1024], replicated, may hold values from 0.1 to 1.9
- w_query: bfloat16 [1024, 1024], P(None, 'tensor')
- w_key: bfloat16 [1024, 1024], P(None, 'tensor')
- w_value: bfloat16 [1024, 1024], P(None, 'tensor'), may hold values from -0.1875 to 0.1875
- w_out: bfloat16 [1024, 1024], P('tensor'), may hold values from -0.1875 to 0.1875
- norm2_gain: float32 [1024], replicated, may hold values from 0.1 to 1.9
- w_point1: bfloat16 [2, 1024, 1024], P(None, None, 'tensor'), may hold values from -0.1875 to 0.1875
- w_depth: float32 [31, 1024], P(None, 'tensor'), may hold values from -1.5 to 1.5
- bn_scale: float32 [1024], P('tensor'), may hold values from 0.1 to 1.9
- bn_shift: float32 [1024], P('tensor'), may hold values from -1 to 1
- w_point2: bfloat16 [1024, 1024], P('tensor'), may hold values from -0.1875 to 0.1875
Outputs:
- output: bfloat16 [4096, 1024], P(('groups', 'context', 'tensor')), parts along dimension 0
There are 2 independent parts, one for each index of `groups`. A program takes and returns all parts, laid end to end along the dimension named above; an argument that names none is the same for every part. Nothing has to cross between parts.
Inputs may be any that keep to these rules, and one draw needn't show every extreme that they name: `frame_valid`: the transcript frames form a prefix of the window of at least 1024 frames, followed by at least one padded frame.
All inputs are finite; a program needn't handle non-finite values.
Results may differ from a plain program's by a relative error of at most 0.0095.
Values may be sent and summed in bfloat16 or wider, within the bound.
A program may use at most 64 MiB of HBM per device.

v0:
```python
import math
import jax
import jax.numpy as jnp
from jax import lax
from jax.sharding import PartitionSpec as P

HD = 64
NEG = -1e30


def with_halo(block, sides, width):
    for axis, dim in sides:
        count = lax.axis_size(axis)
        forward = [(i, i + 1) for i in range(count - 1)]
        backward = [(target, source) for source, target in forward]
        low = lax.ppermute(
            lax.slice_in_dim(block, block.shape[dim] - width, None, axis=dim), axis, forward
        )
        high = lax.ppermute(lax.slice_in_dim(block, 0, width, axis=dim), axis, backward)
        block = jnp.concatenate([low, block, high], axis=dim)
    return block


def normalize(rows, gain):
    values = rows.astype(jnp.float32)
    center = jnp.mean(values, axis=-1, keepdims=True)
    spread = jnp.mean(jnp.square(values - center), axis=-1, keepdims=True)
    return ((values - center) * lax.rsqrt(spread + 1e-05) * gain).astype(jnp.bfloat16)


def local(
    inputs,
    frame_valid,
    norm1_gain,
    w_query,
    w_key,
    w_value,
    w_out,
    norm2_gain,
    w_point1,
    w_depth,
    bn_scale,
    bn_shift,
    w_point2,
):
    frames = inputs.shape[0]
    local_cols = w_query.shape[1]
    head_dim = HD
    heads_here = local_cols // head_dim
    scale = 1.0 / math.sqrt(head_dim)
    normed = normalize(inputs, norm1_gain)
    query = jnp.dot(normed, w_query, preferred_element_type=jnp.float32).astype(jnp.bfloat16)
    query = query.reshape(frames, heads_here, head_dim)
    keys = jnp.dot(normed, w_key, preferred_element_type=jnp.float32).astype(jnp.bfloat16)
    vals = jnp.dot(normed, w_value, preferred_element_type=jnp.float32).astype(jnp.bfloat16)

    def update(carry, key_blk, val_blk, valid_blk):
        run_max, run_sum, accum = carry
        rows = key_blk.shape[0]
        key_heads = key_blk.reshape(rows, heads_here, head_dim)
        val_heads = val_blk.reshape(rows, heads_here, head_dim)
        scores = (
            jnp.einsum("qhd,khd->hqk", query, key_heads, preferred_element_type=jnp.float32) * scale
        )
        live = (valid_blk > 0)[None, None, :]
        scores = jnp.where(live, scores, NEG)
        new_max = jnp.maximum(run_max, jnp.max(scores, axis=-1))
        weights = jnp.where(live, jnp.exp(scores - new_max[:, :, None]), 0.0)
        factor = jnp.exp(run_max - new_max)
        run_sum = run_sum * factor + jnp.sum(weights, axis=-1)
        mixed = jnp.einsum(
            "hqk,khd->qhd",
            weights.astype(jnp.bfloat16),
            val_heads,
            preferred_element_type=jnp.float32,
        )
        accum = accum * jnp.repeat(factor.T, head_dim, axis=1) + mixed.reshape(frames, local_cols)
        return (new_max, run_sum, accum)

    def visit(carry, key_blk, val_blk, valid_blk):
        return update(carry, key_blk, val_blk, valid_blk)

    start_state = (
        jnp.full((heads_here, frames), NEG, jnp.float32),
        jnp.zeros((heads_here, frames), jnp.float32),
        jnp.zeros((frames, local_cols), jnp.float32),
    )
    carry = start_state
    key_part = lax.all_gather(keys, "context", axis=0, tiled=True)
    val_part = lax.all_gather(vals, "context", axis=0, tiled=True)
    valid_part = lax.all_gather(frame_valid, "context", axis=0, tiled=True)
    rows = key_part.shape[0]
    shards = max(rows // frames, 1)
    group = math.gcd(shards, max(1536 // frames, 1))
    blocks = shards // group
    block_rows = rows // blocks

    def advance(state, items):
        return (visit(state, items[0], items[1], items[2]), None)

    stacked = (
        key_part.reshape(blocks, block_rows, local_cols),
        val_part.reshape(blocks, block_rows, local_cols),
        valid_part.reshape(blocks, block_rows),
    )
    carry, unused = lax.scan(advance, carry, stacked)
    run_max, run_sum, accum = carry
    attended = (accum / jnp.repeat(run_sum.T, head_dim, axis=1)).astype(jnp.bfloat16)
    share = frames // lax.axis_size("tensor")
    first_row = lax.axis_index("tensor") * share
    total = lax.psum(jnp.dot(attended, w_out, preferred_element_type=jnp.float32), "tensor")
    residual = (inputs.astype(jnp.float32) + total).astype(jnp.bfloat16)
    normed_two = normalize(residual, norm2_gain)
    residual_rows = lax.dynamic_slice_in_dim(residual, first_row, share, 0)
    value_half = jnp.dot(normed_two, w_point1[0], preferred_element_type=jnp.float32)
    gate_half = jnp.dot(normed_two, w_point1[1], preferred_element_type=jnp.float32)
    gated = jnp.where(
        (frame_valid > 0)[:, None], value_half * jax.nn.sigmoid(gate_half), 0.0
    ).astype(jnp.bfloat16)
    taps = w_depth.shape[0]
    half = (taps - 1) // 2
    padded = with_halo(gated, (("context", 0),), half)
    depth = jnp.zeros((frames, gated.shape[1]), jnp.float32)
    for tap in range(taps):
        depth = depth + padded[tap : tap + frames].astype(jnp.float32) * w_depth[tap]
    activated = jax.nn.silu(depth * bn_scale + bn_shift).astype(jnp.bfloat16)
    conv_rows = lax.psum_scatter(
        jnp.dot(activated, w_point2, preferred_element_type=jnp.float32).astype(jnp.bfloat16),
        "tensor",
        scatter_dimension=0,
        tiled=True,
    ).astype(jnp.float32)
    return (residual_rows.astype(jnp.float32) + conv_rows).astype(jnp.bfloat16)


def solution(mesh):
    placed = (
        P(("groups", "context"), None),
        P(("groups", "context")),
        P(),
        P(None, "tensor"),
        P(None, "tensor"),
        P(None, "tensor"),
        P("tensor", None),
        P(),
        P(None, None, "tensor"),
        P(None, "tensor"),
        P("tensor"),
        P("tensor"),
        P("tensor", None),
    )
    return jax.shard_map(
        local,
        mesh=mesh,
        in_specs=placed,
        out_specs=P(("groups", "context", "tensor"), None),
        check_vma=False,
    )
```

profile of v0, /device:TPU:0, one launch (start us, length us, event | category | flops | bytes accessed | tf_op | source)
XLA Modules:
  0.0 218.2 jit_solution(7202695658550756041)
XLA Ops:
  6.6 1.6 convert_reduce_fusion
  8.2 1.6 fusion.17
  9.9 1.2 convolution_convert_fusion.3
  11.2 1.2 convolution_convert_fusion.1
  12.5 13.7 %all-gather = s32[4,1,512]{2,1,0:T(1,128)S(1)} all-gather(s32[1,1,512]{2,1,0:T(1,128)S(1)} %bitcast.111), channel_id=1, replica_groups=mesh['groups'=2,'context'=4,'tensor'=4] {'context'}, dimensions={0}, use_global_device_ids=true | all-gather | bytes 10240 | tf_op jit(solution)/shard_map/all_gather | solution.py:91
  26.2 1.7 convolution_convert_fusion.2
  27.9 14.0 %all-gather.4.cloned.1.call-done = bf16[2048,256]{1,0:T(8,128)(2,1)} async-done(((bf16[512,256]{1,0:T(8,128)(2,1)}), bf16[2048,256]{1,0:T(8,128)(2,1)}) %all-gather.4.cloned.1.call-update) | async-done | bytes 1048592 | tf_op jit(solution)/shard_map/all_gather | solution.py:89
  41.9 29.0 %all-gather.6.cloned.1.call-done = bf16[2048,256]{1,0:T(8,128)(2,1)} async-done(((bf16[512,256]{1,0:T(8,128)(2,1)}), bf16[2048,256]{1,0:T(8,128)(2,1)}) %all-gather.6.cloned.1.call-update) | async-done | bytes 1048592 | tf_op jit(solution)/shard_map/all_gather | solution.py:90
  70.9 44.4 %while.15 = (s32[]{:T(128)}, f32[4,512]{1,0:T(4,128)S(1)}, f32[4,512]{1,0:T(4,128)S(1)}, f32[512,256]{0,1:T(8,128)S(1)}, s32[4,512]{1,0:T(4,128)S(1)}, /*index=5...) while((s32[]{:T(128)}, f32[4,512]{1,0:T(4,128)S(1)}, ...), condition=%wide.region_5.6_spmd.clone, body=%wide.region_2.5_spmd.clone.sunk | while | flops 282472960 | bytes 17698944 | solution.py:106
  71.0 1.1 constant_dynamic-slice_fusion.3
  72.0 0.1 copy.28
  72.2 2.9 %bitcast_reduce_fusion.2 = (f32[4,512]{1,0:T(4,128)S(1)}, f32[4,512,512]{2,1,0:T(8,128)}) fusion(pred[512]{0:T(512)(128)(4,1)S(1)} %compare_reduce_fusion.2, bf16[512,4,64]{0,2,1:T(8,128)(2,1)S(1)} %bitcast.104, bf16[512,4,64]{0,2,1:T(8,128)(2,1)S(1)} %get-tuple-element.237), kind=kOutput, calls=%fused_computation.1.clone.1 | convolution fusion | flops 137361408 | bytes 4727296 | tf_op jit(solution)/shard_map/while/body/eval_jaxpr/qhd,khd->hqk/dot_general | solution.py:63
  75.1 3.3 %fusion.96 = f32[4,512]{1,0:T(4,128)S(1)} fusion(f32[4,512,512]{2,1,0:T(8,128)} %get-tuple-element.208, f32[4,512]{1,0:T(4,128)S(1)} %get-tuple-element.232, pred[512]{0:T(512)(128)(4,1)S(1)} %compare_reduce_fusion.2), kind=kLoop, calls=%fused_computation.6.clone.1 | loop fusion | flops 5240832 | bytes 4211200 | tf_op jit(solution)/shard_map/while/body/eval_jaxpr/reduce_sum | solution.py:70
  78.4 0.1 copy.29
  78.6 3.3 %fusion.98 = f32[4,64,512]{2,1,0:T(8,128)S(1)} fusion(bf16[512,4,64]{0,2,1:T(8,128)(2,1)S(1)} %bitcast.106, f32[4,512,512]{2,1,0:T(8,128)} %get-tuple-element.208, f32[4,512]{1,0:T(4,128)S(1)} %get-tuple-element.232, pred[512]{0:T(512)(128)(4,1)S(1)} %compare_reduce_fusion.2), kind=kOutput, calls=%fused_computation.7.clone.1 | convolution fusion | flops 139460608 | bytes 4989440 | tf_op jit(solution)/shard_map/while/body/eval_jaxpr/hqk,khd->qhd/dot_general | solution.py:71
  81.8 0.2 bitcast_add_fusion.2
  82.1 1.1 constant_dynamic-slice_fusion.3
  83.1 0.1 copy.28
  83.3 2.9 %bitcast_reduce_fusion.2 = (f32[4,512]{1,0:T(4,128)S(1)}, f32[4,512,512]{2,1,0:T(8,128)}) fusion(pred[512]{0:T(512)(128)(4,1)S(1)} %compare_reduce_fusion.2, bf16[512,4,64]{0,2,1:T(8,128)(2,1)S(1)} %bitcast.104, bf16[512,4,64]{0,2,1:T(8,128)(2,1)S(1)} %get-tuple-element.237), kind=kOutput, calls=%fused_computation.1.clone.1 | convolution fusion | flops 137361408 | bytes 4727296 | tf_op jit(solution)/shard_map/while/body/eval_jaxpr/qhd,khd->hqk/dot_general | solution.py:63
  86.2 3.3 %fusion.96 = f32[4,512]{1,0:T(4,128)S(1)} fusion(f32[4,512,512]{2,1,0:T(8,128)} %get-tuple-element.208, f32[4,512]{1,0:T(4,128)S(1)} %get-tuple-element.232, pred[512]{0:T(512)(128)(4,1)S(1)} %compare_reduce_fusion.2), kind=kLoop, calls=%fused_computation.6.clone.1 | loop fusion | flops 5240832 | bytes 4211200 | tf_op jit(solution)/shard_map/while/body/eval_jaxpr/reduce_sum | solution.py:70
  89.5 0.1 copy.29
  89.7 3.3 %fusion.98 = f32[4,64,512]{2,1,0:T(8,128)S(1)} fusion(bf16[512,4,64]{0,2,1:T(8,128)(2,1)S(1)} %bitcast.106, f32[4,512,512]{2,1,0:T(8,128)} %get-tuple-element.208, f32[4,512]{1,0:T(4,128)S(1)} %get-tuple-element.232, pred[512]{0:T(512)(128)(4,1)S(1)} %compare_reduce_fusion.2), kind=kOutput, calls=%fused_computation.7.clone.1 | convolution fusion | flops 139460608 | bytes 4989440 | tf_op jit(solution)/shard_map/while/body/eval_jaxpr/hqk,khd->qhd/dot_general | solution.py:71
  92.9 0.2 bitcast_add_fusion.2
  93.2 1.1 constant_dynamic-slice_fusion.3
  94.2 0.1 copy.28
  94.4 2.9 %bitcast_reduce_fusion.2 = (f32[4,512]{1,0:T(4,128)S(1)}, f32[4,512,512]{2,1,0:T(8,128)}) fusion(pred[512]{0:T(512)(128)(4,1)S(1)} %compare_reduce_fusion.2, bf16[512,4,64]{0,2,1:T(8,128)(2,1)S(1)} %bitcast.104, bf16[512,4,64]{0,2,1:T(8,128)(2,1)S(1)} %get-tuple-element.237), kind=kOutput, calls=%fused_computation.1.clone.1 | convolution fusion | flops 137361408 | bytes 4727296 | tf_op jit(solution)/shard_map/while/body/eval_jaxpr/qhd,khd->hqk/dot_general | solution.py:63
  97.3 3.3 %fusion.96 = f32[4,512]{1,0:T(4,128)S(1)} fusion(f32[4,512,512]{2,1,0:T(8,128)} %get-tuple-element.208, f32[4,512]{1,0:T(4,128)S(1)} %get-tuple-element.232, pred[512]{0:T(512)(128)(4,1)S(1)} %compare_reduce_fusion.2), kind=kLoop, calls=%fused_computation.6.clone.1 | loop fusion | flops 5240832 | bytes 4211200 | tf_op jit(solution)/shard_map/while/body/eval_jaxpr/reduce_sum | solution.py:70
  100.6 0.1 copy.29
  100.8 3.3 %fusion.98 = f32[4,64,512]{2,1,0:T(8,128)S(1)} fusion(bf16[512,4,64]{0,2,1:T(8,128)(2,1)S(1)} %bitcast.106, f32[4,512,512]{2,1,0:T(8,128)} %get-tuple-element.208, f32[4,512]{1,0:T(4,128)S(1)} %get-tuple-element.232, pred[512]{0:T(512)(128)(4,1)S(1)} %compare_reduce_fusion.2), kind=kOutput, calls=%fused_computation.7.clone.1 | convolution fusion | flops 139460608 | bytes 4989440 | tf_op jit(solution)/shard_map/while/body/eval_jaxpr/hqk,khd->qhd/dot_general | solution.py:71
  104.1 0.2 bitcast_add_fusion.2
  104.3 1.1 constant_dynamic-slice_fusion.3
  105.3 0.1 copy.28
  105.5 2.9 %bitcast_reduce_fusion.2 = (f32[4,512]{1,0:T(4,128)S(1)}, f32[4,512,512]{2,1,0:T(8,128)}) fusion(pred[512]{0:T(512)(128)(4,1)S(1)} %compare_reduce_fusion.2, bf16[512,4,64]{0,2,1:T(8,128)(2,1)S(1)} %bitcast.104, bf16[512,4,64]{0,2,1:T(8,128)(2,1)S(1)} %get-tuple-element.237), kind=kOutput, calls=%fused_computation.1.clone.1 | convolution fusion | flops 137361408 | bytes 4727296 | tf_op jit(solution)/shard_map/while/body/eval_jaxpr/qhd,khd->hqk/dot_general | solution.py:63
  108.4 3.3 %fusion.96 = f32[4,512]{1,0:T(4,128)S(1)} fusion(f32[4,512,512]{2,1,0:T(8,128)} %get-tuple-element.208, f32[4,512]{1,0:T(4,128)S(1)} %get-tuple-element.232, pred[512]{0:T(512)(128)(4,1)S(1)} %compare_reduce_fusion.2), kind=kLoop, calls=%fused_computation.6.clone.1 | loop fusion | flops 5240832 | bytes 4211200 | tf_op jit(solution)/shard_map/while/body/eval_jaxpr/reduce_sum | solution.py:70
  111.9 3.3 %fusion.98 = f32[4,64,512]{2,1,0:T(8,128)S(1)} fusion(bf16[512,4,64]{0,2,1:T(8,128)(2,1)S(1)} %bitcast.106, f32[4,512,512]{2,1,0:T(8,128)} %get-tuple-element.208, f32[4,512]{1,0:T(4,128)S(1)} %get-tuple-element.232, pred[512]{0:T(512)(128)(4,1)S(1)} %compare_reduce_fusion.2), kind=kOutput, calls=%fused_computation.7.clone.1 | convolution fusion | flops 139460608 | bytes 4989440 | tf_op jit(solution)/shard_map/while/body/eval_jaxpr/hqk,khd->qhd/dot_general | solution.py:71
  115.2 0.2 bitcast_add_fusion.2
  115.4 1.8 fusion.73
  117.4 50.9 %all-reduce.2.cloned.1.call-done = f32[512,1024]{1,0:T(8,128)} async-done(((f32[512,1024]{1,0:T(8,128)}), f32[512,1024]{1,0:T(8,128)}) %all-reduce.2.cloned.1.call-update) | async-done | bytes 2097168 | tf_op jit(solution)/shard_map/psum | solution.py:111
  168.3 2.0 convert_reduce_fusion.1
  170.3 0.4 fusion.20
  170.7 0.5 fusion.27
  171.3 0.5 fusion.28
  171.9 1.3 collective-permute-start.1
  173.2 4.5 %collective-permute-start = (bf16[15,256]{1,0:T(8,128)(2,1)S(1)}, bf16[15,256]{1,0:T(8,128)(2,1)S(1)}, u32[]{:S(2)}, u32[]{:S(2)}) collective-permute-start(bf16[15,256]{1,0:T(8,128)(2,1)S(1)} %get-tuple-element.117), channel_id=1, source_target_pairs={{0,4},{4,8},{8,12},{1,5},{5,9},{9,13},{2,6},{6,10},{10,14},{3,7},{... | collective-permute-start | bytes 23048 | tf_op jit(solution)/shard_map/ppermute | solution.py:16
  177.7 1.3 collective-permute-done
  179.1 4.9 %convolution_convert_fusion = bf16[512,1024]{1,0:T(8,128)(2,1)} fusion(bf16[256,1024]{1,0:T(8,128)(2,1)S(1)} %copy-done.7, bf16[512,256]{1,0:T(8,128)(2,1)S(1)} %fusion.28, bf16[15,256]{1,0:T(8,128)(2,1)S(1)} %collective-permute-done.1, bf16[15,256]{1,0:T(8,128)(2,1)S(1)} %collective-permute-done, f32[256]{0:T(256)S(1)} %copy-done.10, ...), kind=kOutput, calls=%fused_computation.67 | convolution fusion | flops 293732352 | bytes 1884160 | tf_op jit(solution)/shard_map/dot_general | solution.py:128
  184.0 26.0 %reduce-scatter.2.cloned.1.call-done = bf16[128,1024]{1,0:T(8,128)(2,1)} async-done(((bf16[512,1024]{1,0:T(8,128)(2,1)}), bf16[128,1024]{1,0:T(8,128)(2,1)}) %reduce-scatter.2.cloned.1.call-update) | async-done | bytes 262160 | tf_op jit(solution)/shard_map/reduce_scatter | solution.py:127
  209.9 1.7 add_convert_fusion
  (63 shorter events, 0.8 us)
Async XLA Ops:
  6.5 108.9 %copy-start = (bf16[256,1024]{1,0:T(8,128)(2,1)S(1)}, bf16[256,1024]{1,0:T(8,128)(2,1)}, u32[]{:S(2)}) copy-start(bf16[256,1024]{1,0:T(8,128)(2,1)} %param.21) | copy-start | bytes 1572868
  6.5 3.3 %copy-start.1 = (bf16[512,1024]{1,0:T(8,128)(2,1)S(1)}, bf16[512,1024]{1,0:T(8,128)(2,1)}, u32[]{:S(2)}) copy-start(bf16[512,1024]{1,0:T(8,128)(2,1)} %param.15) | copy-start | bytes 3145732
  6.5 3.3 %copy-start.5 = (bf16[1024,256]{1,0:T(8,128)(2,1)S(1)}, bf16[1024,256]{1,0:T(8,128)(2,1)}, u32[]{:S(2)}) copy-start(bf16[1024,256]{1,0:T(8,128)(2,1)} %param.19) | copy-start | bytes 1572868
  6.5 3.3 %copy-start.8 = (f32[1024]{0:T(1024)S(1)}, f32[1024]{0:T(1024)}, u32[]{:S(2)}) copy-start(f32[1024]{0:T(1024)} %param.17) | copy-start | bytes 12292
  6.5 35.4 %all-gather.4.cloned.1.call-start = ((), (), s32[]{:S(2)}) async-start(), calls=%async_computation.1 | async-start | bytes 1310720 | tf_op jit(solution)/shard_map/all_gather | solution.py:89
  9.8 1.4 copy-start.6
  11.1 1.4 copy-start.3
  11.1 59.8 %all-gather.6.cloned.1.call-start = ((), (), s32[]{:S(2)}) async-start(), calls=%async_computation.2 | async-start | bytes 1310720 | tf_op jit(solution)/shard_map/all_gather | solution.py:90
  12.4 155.9 %all-reduce.2.cloned.1.call-start = ((), (), s32[]{:S(2)}) async-start(), calls=%async_computation.3 | async-start | bytes 4194304 | tf_op jit(solution)/shard_map/psum | solution.py:111
  115.4 1.9 copy-start.2
  117.2 92.7 %reduce-scatter.2.cloned.1.call-start = ((), (), s32[]{:S(2)}) async-start(), calls=%async_computation.4 | async-start | bytes 1310720 | tf_op jit(solution)/shard_map/reduce_scatter | solution.py:127
  117.3 53.4 %copy-start.9 = (f32[1024]{0:T(1024)S(1)}, f32[1024]{0:T(1024)}, u32[]{:S(2)}) copy-start(f32[1024]{0:T(1024)} %param.22) | copy-start | bytes 12292
  168.3 2.4 %copy-start.4 = (bf16[2,1024,256]{2,1,0:T(8,128)(2,1)S(1)}, bf16[2,1024,256]{2,1,0:T(8,128)(2,1)}, u32[]{:S(2)}) copy-start(bf16[2,1024,256]{2,1,0:T(8,128)(2,1)} %param.23) | copy-start | bytes 3145732
  171.3 7.8 %copy-start.7 = (bf16[256,1024]{1,0:T(8,128)(2,1)S(1)}, bf16[256,1024]{1,0:T(8,128)(2,1)}, u32[]{:S(2)}) copy-start(bf16[256,1024]{1,0:T(8,128)(2,1)} %param.27) | copy-start | bytes 1572868
  171.3 7.8 %copy-start.10 = (f32[256]{0:T(256)S(1)}, f32[256]{0:T(256)}, u32[]{:S(2)}) copy-start(f32[256]{0:T(256)} %param.26) | copy-start | bytes 3076
  171.3 7.8 %copy-start.11 = (f32[256]{0:T(256)S(1)}, f32[256]{0:T(256)}, u32[]{:S(2)}) copy-start(f32[256]{0:T(256)} %param.25) | copy-start | bytes 3076
  171.9 5.9 %collective-permute-start.1 = (bf16[15,256]{1,0:T(8,128)(2,1)S(1)}, bf16[15,256]{1,0:T(8,128)(2,1)S(1)}, u32[]{:S(2)}, u32[]{:S(2)}) collective-permute-start(bf16[15,256]{1,0:T(8,128)(2,1)S(1)} %get-tuple-element.118), channel_id=1, source_target_pairs={{4,0},{8,4},{12,8},{5,1},{9,5},{13,9},{6,2},{10,6},{14,10},{7,3},{... | collective-permute-start | bytes 23048 | tf_op jit(solution)/shard_map/ppermute | solution.py:19
  173.2 5.9 %collective-permute-start = (bf16[15,256]{1,0:T(8,128)(2,1)S(1)}, bf16[15,256]{1,0:T(8,128)(2,1)S(1)}, u32[]{:S(2)}, u32[]{:S(2)}) collective-permute-start(bf16[15,256]{1,0:T(8,128)(2,1)S(1)} %get-tuple-element.117), channel_id=1, source_target_pairs={{0,4},{4,8},{8,12},{1,5},{5,9},{9,13},{2,6},{6,10},{10,14},{3,7},{... | collective-permute-start | bytes 23048 | tf_op jit(solution)/shard_map/ppermute | solution.py:16
Sparse Core Ops, SparseCore 0:
  11.2 30.6 all-gather.3
  43.5 27.3 all-gather.5
  117.4 50.8 all-reduce.1
  184.1 25.8 reduce-scatter.1
where the time goes:
time: 219 us; the launch traced here: 218 us
  waiting for transfers between devices  121 us (55%)
  matrix products  36.7 us (17%)
  other arithmetic  21.4 us (10%)
  blocking collectives  13.7 us (6%)
  between operations  13.4 us (6%)
  starting transfers between devices  6 us (3%)
  local copies, waits for them, and re-layouts  5.5 us (3%)
    psum x1, waiting for transfers between devices, local(): lax.psum(jnp.dot(attended, w_out, preferred_element_type=jnp.float32), 't...  50.9 us
    all_gather x1, waiting for transfers between devices, local(): val_part = lax.all_gather(vals, 'context', axis=0, tiled=True)  29 us
    reduce_scatter x1, waiting for transfers between devices, local(): lax.psum_scatter(jnp.dot(activated, w_point2, preferred_element_type=jnp....  26 us
    all_gather x1, waiting for transfers between devices, local(): key_part = lax.all_gather(keys, 'context', axis=0, tiled=True)  14 us
    all_gather x1, blocking collectives, local(): valid_part = lax.all_gather(frame_valid, 'context', axis=0, tiled=True)  13.7 us
    dot_general x4, matrix products, update(): jnp.einsum('hqk,khd->qhd', weights.astype(jnp.bfloat16), val_heads, prefe...  13.1 us
    reduce_sum x4, other arithmetic, update(): run_sum = run_sum * factor + jnp.sum(weights, axis=-1)  13.1 us
    dot_general x4, matrix products, update(): jnp.einsum('qhd,khd->hqk', query, key_heads, preferred_element_type=jnp.f...  11.6 us
  transfers between devices with their start and end apart: 6, of which 5 were waited for; matrix products, arithmetic and copies ran while one was open for 1% of the time, Pallas kernels for 0%

commit v1 on v0

--- a/solution.py
+++ b/solution.py
@@ -87,7 +87,16 @@
     )
     carry = start_state
     key_part = lax.all_gather(keys, "context", axis=0, tiled=True)
-    val_part = lax.all_gather(vals, "context", axis=0, tiled=True)
+    ways = lax.axis_size("context")
+    up = [(d, (d + 1) % ways) for d in range(ways)]
+    down = [(d, (d - 1) % ways) for d in range(ways)]
+    earlier, later = ([vals], [vals])
+    for _ in range(ways // 2):
+        earlier.append(lax.ppermute(earlier[-1], "context", up))
+    for _ in range((ways - 1) // 2):
+        later.append(lax.ppermute(later[-1], "context", down))
+    line = jnp.concatenate([*earlier[::-1], *later[1:]], axis=0)
+    val_part = jnp.roll(line, (lax.axis_index("context") - ways // 2) * vals.shape[0], axis=0)
     valid_part = lax.all_gather(frame_valid, "context", axis=0, tiled=True)
     rows = key_part.shape[0]
     shards = max(rows // frames, 1)

time: 219 us -> 199 us (0.909)
  waiting for transfers between devices: 121 us -> 89.3 us
  blocking collectives: 13.7 us -> 20.1 us
  starting transfers between devices: 6 us -> 11.2 us
    all_gather x1 -> x0, waiting for transfers between devices: 29 us -> none  [local(): val_part = lax.all_gather(vals, 'context', axis=0, tiled=True)]
    all_gather x1, waiting for transfers between devices: 14 us -> 0.01 us  [local(): key_part = lax.all_gather(keys, 'context', axis=0, tiled=True)]
    ppermute x0 -> x3, waiting for transfers between devices: none -> 11.2 us  [the longest x2 11.2 us: local(): earlier.append(lax.ppermute(earlier[-1], 'context', up))]
    all_gather x1, blocking collectives: 13.7 us -> 20.1 us  [local(): valid_part = lax.all_gather(frame_valid, 'context', axis=0, tiled=True)]
    ppermute x0 -> x3, starting transfers between devices: none -> 5.29 us  [the longest x2 3.19 us: local(): earlier.append(lax.ppermute(earlier[-1], 'context', up))]
  transfers between devices with their start and end apart: 6 -> 8, of which waited for: 5 -> 4; matrix products, arithmetic and copies ran while one was open for 1% -> 2% of each run, Pallas kernels for 0% -> 0%
where the time goes in v1:
time: 199 us
  waiting for transfers between devices  89.3 us (45%)
  matrix products  36 us (18%)
  other arithmetic  21.5 us (11%)
  blocking collectives  20.1 us (10%)
  between operations  13.4 us (7%)
  starting transfers between devices  11.2 us (6%)
  local copies, waits for them, and re-layouts  6.74 us (3%)
    psum x1, waiting for transfers between devices, local(): lax.psum(jnp.dot(attended, w_out, preferred_element_type=jnp.float32), 't...  50.7 us
    reduce_scatter x1, waiting for transfers between devices, local(): lax.psum_scatter(jnp.dot(activated, w_point2, preferred_element_type=jnp....  26 us
    all_gather x1, blocking collectives, local(): valid_part = lax.all_gather(frame_valid, 'context', axis=0, tiled=True)  20.1 us
    dot_general x4, matrix products, update(): jnp.einsum('hqk,khd->qhd', weights.astype(jnp.bfloat16), val_heads, prefe...  13.1 us
    reduce_sum x4, other arithmetic, update(): run_sum = run_sum * factor + jnp.sum(weights, axis=-1)  13.1 us
    dot_general x4, matrix products, update(): jnp.einsum('qhd,khd->hqk', query, key_heads, preferred_element_type=jnp.f...  11.6 us
    ppermute x2, waiting for transfers between devices, local(): earlier.append(lax.ppermute(earlier[-1], 'context', up))  11.2 us
    dynamic_slice x12, local copies, waits for them, and re-layouts, local(): carry, unused = lax.scan(advance, carry, stacked)  5.39 us
  transfers between devices with their start and end apart: 8, of which 4 were waited for; matrix products, arithmetic and copies ran while one was open for 2% of the time, Pallas kernels for 0%

profile of v1, /device:TPU:0, one launch (start us, length us, event | category | flops | bytes accessed | tf_op | source)
XLA Modules:
  0.0 198.5 jit_solution(17826209684897552156)
XLA Ops:
  6.6 1.6 convert_reduce_fusion
  8.2 1.7 fusion.17
  9.9 0.5 convolution_convert_fusion.1
  10.4 3.1 %collective-permute-start = (bf16[512,256]{1,0:T(8,128)(2,1)S(1)}, bf16[512,256]{1,0:T(8,128)(2,1)S(1)}, u32[]{:S(2)}, u32[]{:S(2)}) collective-permute-start(bf16[512,256]{1,0:T(8,128)(2,1)S(1)} %convolution_convert_fusion.1), channel_id=1, source_target_pairs={{0,4},{4,8},{8,12},{12,0},{1,5},{5,9},{9,13},{13,1},{2,6},{6,10},{... | collective-permute-start | bytes 786440 | tf_op jit(solution)/shard_map/ppermute | solution.py:95
  13.5 1.2 convolution_convert_fusion.3
  14.8 2.1 %collective-permute-start.2 = (bf16[512,256]{1,0:T(8,128)(2,1)S(1)}, bf16[512,256]{1,0:T(8,128)(2,1)S(1)}, u32[]{:S(2)}, u32[]{:S(2)}) collective-permute-start(bf16[512,256]{1,0:T(8,128)(2,1)S(1)} %convolution_convert_fusion.1), channel_id=1, source_target_pairs={{0,12},{4,0},{8,4},{12,8},{1,13},{5,1},{9,5},{13,9},{2,14},{6,2},{... | collective-permute-start | bytes 786440 | tf_op jit(solution)/shard_map/ppermute | solution.py:97
  16.9 20.1 %all-gather = s32[4,1,512]{2,1,0:T(1,128)S(1)} all-gather(s32[1,1,512]{2,1,0:T(1,128)S(1)} %bitcast.111), channel_id=1, replica_groups=mesh['groups'=2,'context'=4,'tensor'=4] {'context'}, dimensions={0}, use_global_device_ids=true | all-gather | bytes 10240 | tf_op jit(solution)/shard_map/all_gather | solution.py:100
  37.2 1.7 convolution_convert_fusion.2
  38.9 11.2 %collective-permute-done.1 = bf16[512,256]{1,0:T(8,128)(2,1)S(1)} collective-permute-done((bf16[512,256]{1,0:T(8,128)(2,1)S(1)}, bf16[512,256]{1,0:T(8,128)(2,1)S(1)}, u32[]{:S(2)}, u32[]{:S(2)}) %collective-permute-start.1) | collective-permute-done | bytes 262176 | tf_op jit(solution)/shard_map/ppermute | solution.py:95
  50.4 1.1 constant_dynamic-slice_fusion.2
  51.5 44.4 %while.15 = (s32[]{:T(128)}, f32[4,512]{1,0:T(4,128)S(1)}, f32[4,512]{1,0:T(4,128)S(1)}, f32[512,256]{0,1:T(8,128)S(1)}, s32[4,512]{1,0:T(4,128)S(1)}, /*index=5...) while((s32[]{:T(128)}, f32[4,512]{1,0:T(4,128)S(1)}, ...), condition=%wide.region_5.6_spmd.clone, body=%wide.region_2.5_spmd.clone.sunk | while | flops 282472960 | bytes 17698944 | solution.py:115
  51.5 1.1 constant_dynamic-slice_fusion.4
  52.6 0.1 copy.30
  52.7 2.9 %bitcast_reduce_fusion.2 = (f32[4,512]{1,0:T(4,128)S(1)}, f32[4,512,512]{2,1,0:T(8,128)}) fusion(pred[512]{0:T(512)(128)(4,1)S(1)} %compare_reduce_fusion.2, bf16[512,4,64]{0,2,1:T(8,128)(2,1)S(1)} %bitcast.104, bf16[512,4,64]{0,2,1:T(8,128)(2,1)S(1)} %get-tuple-element.245), kind=kOutput, calls=%fused_computation.1.clone.1 | convolution fusion | flops 137361408 | bytes 4727296 | tf_op jit(solution)/shard_map/while/body/eval_jaxpr/qhd,khd->hqk/dot_general | solution.py:63
  55.6 3.3 %fusion.96 = f32[4,512]{1,0:T(4,128)S(1)} fusion(f32[4,512,512]{2,1,0:T(8,128)} %get-tuple-element.216, f32[4,512]{1,0:T(4,128)S(1)} %get-tuple-element.240, pred[512]{0:T(512)(128)(4,1)S(1)} %compare_reduce_fusion.2), kind=kLoop, calls=%fused_computation.6.clone.1 | loop fusion | flops 5240832 | bytes 4211200 | tf_op jit(solution)/shard_map/while/body/eval_jaxpr/reduce_sum | solution.py:70
  58.9 0.1 copy.31
  59.1 3.3 %fusion.98 = f32[4,64,512]{2,1,0:T(8,128)S(1)} fusion(bf16[512,4,64]{0,2,1:T(8,128)(2,1)S(1)} %bitcast.106, f32[4,512,512]{2,1,0:T(8,128)} %get-tuple-element.216, f32[4,512]{1,0:T(4,128)S(1)} %get-tuple-element.240, pred[512]{0:T(512)(128)(4,1)S(1)} %compare_reduce_fusion.2), kind=kOutput, calls=%fused_computation.7.clone.1 | convolution fusion | flops 139460608 | bytes 4989440 | tf_op jit(solution)/shard_map/while/body/eval_jaxpr/hqk,khd->qhd/dot_general | solution.py:71
  62.4 0.2 bitcast_add_fusion.2
  62.6 1.1 constant_dynamic-slice_fusion.4
  63.7 0.1 copy.30
  63.8 2.9 %bitcast_reduce_fusion.2 = (f32[4,512]{1,0:T(4,128)S(1)}, f32[4,512,512]{2,1,0:T(8,128)}) fusion(pred[512]{0:T(512)(128)(4,1)S(1)} %compare_reduce_fusion.2, bf16[512,4,64]{0,2,1:T(8,128)(2,1)S(1)} %bitcast.104, bf16[512,4,64]{0,2,1:T(8,128)(2,1)S(1)} %get-tuple-element.245), kind=kOutput, calls=%fused_computation.1.clone.1 | convolution fusion | flops 137361408 | bytes 4727296 | tf_op jit(solution)/shard_map/while/body/eval_jaxpr/qhd,khd->hqk/dot_general | solution.py:63
  66.7 3.3 %fusion.96 = f32[4,512]{1,0:T(4,128)S(1)} fusion(f32[4,512,512]{2,1,0:T(8,128)} %get-tuple-element.216, f32[4,512]{1,0:T(4,128)S(1)} %get-tuple-element.240, pred[512]{0:T(512)(128)(4,1)S(1)} %compare_reduce_fusion.2), kind=kLoop, calls=%fused_computation.6.clone.1 | loop fusion | flops 5240832 | bytes 4211200 | tf_op jit(solution)/shard_map/while/body/eval_jaxpr/reduce_sum | solution.py:70
  70.2 3.3 %fusion.98 = f32[4,64,512]{2,1,0:T(8,128)S(1)} fusion(bf16[512,4,64]{0,2,1:T(8,128)(2,1)S(1)} %bitcast.106, f32[4,512,512]{2,1,0:T(8,128)} %get-tuple-element.216, f32[4,512]{1,0:T(4,128)S(1)} %get-tuple-element.240, pred[512]{0:T(512)(128)(4,1)S(1)} %compare_reduce_fusion.2), kind=kOutput, calls=%fused_computation.7.clone.1 | convolution fusion | flops 139460608 | bytes 4989440 | tf_op jit(solution)/shard_map/while/body/eval_jaxpr/hqk,khd->qhd/dot_general | solution.py:71
  73.5 0.2 bitcast_add_fusion.2
  73.7 1.1 constant_dynamic-slice_fusion.4
  74.9 2.9 %bitcast_reduce_fusion.2 = (f32[4,512]{1,0:T(4,128)S(1)}, f32[4,512,512]{2,1,0:T(8,128)}) fusion(pred[512]{0:T(512)(128)(4,1)S(1)} %compare_reduce_fusion.2, bf16[512,4,64]{0,2,1:T(8,128)(2,1)S(1)} %bitcast.104, bf16[512,4,64]{0,2,1:T(8,128)(2,1)S(1)} %get-tuple-element.245), kind=kOutput, calls=%fused_computation.1.clone.1 | convolution fusion | flops 137361408 | bytes 4727296 | tf_op jit(solution)/shard_map/while/body/eval_jaxpr/qhd,khd->hqk/dot_general | solution.py:63
  77.9 3.3 %fusion.96 = f32[4,512]{1,0:T(4,128)S(1)} fusion(f32[4,512,512]{2,1,0:T(8,128)} %get-tuple-element.216, f32[4,512]{1,0:T(4,128)S(1)} %get-tuple-element.240, pred[512]{0:T(512)(128)(4,1)S(1)} %compare_reduce_fusion.2), kind=kLoop, calls=%fused_computation.6.clone.1 | loop fusion | flops 5240832 | bytes 4211200 | tf_op jit(solution)/shard_map/while/body/eval_jaxpr/reduce_sum | solution.py:70
  81.2 0.1 copy.31
  81.3 3.3 %fusion.98 = f32[4,64,512]{2,1,0:T(8,128)S(1)} fusion(bf16[512,4,64]{0,2,1:T(8,128)(2,1)S(1)} %bitcast.106, f32[4,512,512]{2,1,0:T(8,128)} %get-tuple-element.216, f32[4,512]{1,0:T(4,128)S(1)} %get-tuple-element.240, pred[512]{0:T(512)(128)(4,1)S(1)} %compare_reduce_fusion.2), kind=kOutput, calls=%fused_computation.7.clone.1 | convolution fusion | flops 139460608 | bytes 4989440 | tf_op jit(solution)/shard_map/while/body/eval_jaxpr/hqk,khd->qhd/dot_general | solution.py:71
  84.6 0.2 bitcast_add_fusion.2
  84.8 1.1 constant_dynamic-slice_fusion.4
  85.9 0.1 copy.30
  86.0 2.9 %bitcast_reduce_fusion.2 = (f32[4,512]{1,0:T(4,128)S(1)}, f32[4,512,512]{2,1,0:T(8,128)}) fusion(pred[512]{0:T(512)(128)(4,1)S(1)} %compare_reduce_fusion.2, bf16[512,4,64]{0,2,1:T(8,128)(2,1)S(1)} %bitcast.104, bf16[512,4,64]{0,2,1:T(8,128)(2,1)S(1)} %get-tuple-element.245), kind=kOutput, calls=%fused_computation.1.clone.1 | convolution fusion | flops 137361408 | bytes 4727296 | tf_op jit(solution)/shard_map/while/body/eval_jaxpr/qhd,khd->hqk/dot_general | solution.py:63
  89.0 3.3 %fusion.96 = f32[4,512]{1,0:T(4,128)S(1)} fusion(f32[4,512,512]{2,1,0:T(8,128)} %get-tuple-element.216, f32[4,512]{1,0:T(4,128)S(1)} %get-tuple-element.240, pred[512]{0:T(512)(128)(4,1)S(1)} %compare_reduce_fusion.2), kind=kLoop, calls=%fused_computation.6.clone.1 | loop fusion | flops 5240832 | bytes 4211200 | tf_op jit(solution)/shard_map/while/body/eval_jaxpr/reduce_sum | solution.py:70
  92.4 3.3 %fusion.98 = f32[4,64,512]{2,1,0:T(8,128)S(1)} fusion(bf16[512,4,64]{0,2,1:T(8,128)(2,1)S(1)} %bitcast.106, f32[4,512,512]{2,1,0:T(8,128)} %get-tuple-element.216, f32[4,512]{1,0:T(4,128)S(1)} %get-tuple-element.240, pred[512]{0:T(512)(128)(4,1)S(1)} %compare_reduce_fusion.2), kind=kOutput, calls=%fused_computation.7.clone.1 | convolution fusion | flops 139460608 | bytes 4989440 | tf_op jit(solution)/shard_map/while/body/eval_jaxpr/hqk,khd->qhd/dot_general | solution.py:71
  95.7 0.2 bitcast_add_fusion.2
  96.0 1.8 fusion.73
  97.9 50.7 %all-reduce.2.cloned.1.call-done = f32[512,1024]{1,0:T(8,128)} async-done(((f32[512,1024]{1,0:T(8,128)}), f32[512,1024]{1,0:T(8,128)}) %all-reduce.2.cloned.1.call-update) | async-done | bytes 2097168 | tf_op jit(solution)/shard_map/psum | solution.py:120
  148.6 2.0 %convert_reduce_fusion.1 = (f32[512]{0:T(512)S(1)}, bf16[512,1024]{1,0:T(8,128)(2,1)S(1)}) fusion(f32[512,1024]{1,0:T(8,128)} %all-reduce.2.cloned.1.call-done, bf16[512,1024]{1,0:T(8,128)(2,1)S(1)} %copy-done.1), kind=kLoop, calls=%fused_computation.27 | loop fusion | flops 2620928 | bytes 4196352 | tf_op jit(solution)/shard_map/reduce_sum | solution.py:26
  150.6 0.4 fusion.20
  151.1 0.5 fusion.27
  151.6 0.5 fusion.28
  152.2 1.3 collective-permute-start.4
  153.5 4.5 %collective-permute-start.3 = (bf16[15,256]{1,0:T(8,128)(2,1)S(1)}, bf16[15,256]{1,0:T(8,128)(2,1)S(1)}, u32[]{:S(2)}, u32[]{:S(2)}) collective-permute-start(bf16[15,256]{1,0:T(8,128)(2,1)S(1)} %get-tuple-element.125), channel_id=1, source_target_pairs={{0,4},{4,8},{8,12},{1,5},{5,9},{9,13},{2,6},{6,10},{10,14},{3,7},{... | collective-permute-start | bytes 23048 | tf_op jit(solution)/shard_map/ppermute | solution.py:16
  158.1 1.3 collective-permute-done.3
  159.4 4.9 %convolution_convert_fusion = bf16[512,1024]{1,0:T(8,128)(2,1)} fusion(bf16[256,1024]{1,0:T(8,128)(2,1)S(1)} %copy-done.7, bf16[512,256]{1,0:T(8,128)(2,1)S(1)} %fusion.28, bf16[15,256]{1,0:T(8,128)(2,1)S(1)} %collective-permute-done.4, bf16[15,256]{1,0:T(8,128)(2,1)S(1)} %collective-permute-done.3, f32[256]{0:T(256)S(1)} %copy-done.10, ...), kind=kOutput, calls=%fused_computation.67 | convolution fusion | flops 293732352 | bytes 1884160 | tf_op jit(solution)/shard_map/dot_general | solution.py:137
  164.3 26.0 %reduce-scatter.2.cloned.1.call-done = bf16[128,1024]{1,0:T(8,128)(2,1)} async-done(((bf16[512,1024]{1,0:T(8,128)(2,1)}), bf16[128,1024]{1,0:T(8,128)(2,1)}) %reduce-scatter.2.cloned.1.call-update) | async-done | bytes 262160 | tf_op jit(solution)/shard_map/reduce_scatter | solution.py:136
  190.3 1.7 add_convert_fusion
  (75 shorter events, 1.3 us)
Async XLA Ops:
  6.5 89.4 %copy-start = (bf16[256,1024]{1,0:T(8,128)(2,1)S(1)}, bf16[256,1024]{1,0:T(8,128)(2,1)}, u32[]{:S(2)}) copy-start(bf16[256,1024]{1,0:T(8,128)(2,1)} %param.21) | copy-start | bytes 1572868
  6.5 3.3 %copy-start.1 = (bf16[512,1024]{1,0:T(8,128)(2,1)S(1)}, bf16[512,1024]{1,0:T(8,128)(2,1)}, u32[]{:S(2)}) copy-start(bf16[512,1024]{1,0:T(8,128)(2,1)} %param.15) | copy-start | bytes 3145732
  6.5 3.4 %copy-start.8 = (f32[1024]{0:T(1024)S(1)}, f32[1024]{0:T(1024)}, u32[]{:S(2)}) copy-start(f32[1024]{0:T(1024)} %param.17) | copy-start | bytes 12292
  6.5 3.4 %copy-start.5 = (bf16[1024,256]{1,0:T(8,128)(2,1)S(1)}, bf16[1024,256]{1,0:T(8,128)(2,1)}, u32[]{:S(2)}) copy-start(bf16[1024,256]{1,0:T(8,128)(2,1)} %param.20) | copy-start | bytes 1572868
  6.5 44.9 %all-gather.3.cloned.1.call-start = ((), (), s32[]{:S(2)}) async-start(), calls=%async_computation.1 | async-start | bytes 1310720 | tf_op jit(solution)/shard_map/all_gather | solution.py:89
  8.2 5.4 %copy-start.6 = (bf16[1024,256]{1,0:T(8,128)(2,1)S(1)}, bf16[1024,256]{1,0:T(8,128)(2,1)}, u32[]{:S(2)}) copy-start(bf16[1024,256]{1,0:T(8,128)(2,1)} %param.19) | copy-start | bytes 1572868
  10.4 6.5 %copy-start.3 = (s32[512]{0:T(512)S(1)}, s32[512]{0:T(512)}, u32[]{:S(2)}) copy-start(s32[512]{0:T(512)} %param.16) | copy-start | bytes 6148
  10.4 26.6 %collective-permute-start = (bf16[512,256]{1,0:T(8,128)(2,1)S(1)}, bf16[512,256]{1,0:T(8,128)(2,1)S(1)}, u32[]{:S(2)}, u32[]{:S(2)}) collective-permute-start(bf16[512,256]{1,0:T(8,128)(2,1)S(1)} %convolution_convert_fusion.1), channel_id=1, source_target_pairs={{0,4},{4,8},{8,12},{12,0},{1,5},{5,9},{9,13},{13,1},{2,6},{6,10},{... | collective-permute-start | bytes 786440 | tf_op jit(solution)/shard_map/ppermute | solution.py:95
  14.8 133.8 %all-reduce.2.cloned.1.call-start = ((), (), s32[]{:S(2)}) async-start(), calls=%async_computation.2 | async-start | bytes 4194304 | tf_op jit(solution)/shard_map/psum | solution.py:120
  14.8 35.4 %collective-permute-start.2 = (bf16[512,256]{1,0:T(8,128)(2,1)S(1)}, bf16[512,256]{1,0:T(8,128)(2,1)S(1)}, u32[]{:S(2)}, u32[]{:S(2)}) collective-permute-start(bf16[512,256]{1,0:T(8,128)(2,1)S(1)} %convolution_convert_fusion.1), channel_id=1, source_target_pairs={{0,12},{4,0},{8,4},{12,8},{1,13},{5,1},{9,5},{13,9},{2,14},{6,2},{... | collective-permute-start | bytes 786440 | tf_op jit(solution)/shard_map/ppermute | solution.py:97
  37.1 13.1 %collective-permute-start.1 = (bf16[512,256]{1,0:T(8,128)(2,1)S(1)}, bf16[512,256]{1,0:T(8,128)(2,1)S(1)}, u32[]{:S(2)}, u32[]{:S(2)}) collective-permute-start(bf16[512,256]{1,0:T(8,128)(2,1)S(1)} %collective-permute-done), channel_id=1, source_target_pairs={{0,4},{4,8},{8,12},{12,0},{1,5},{5,9},{9,13},{13,1},{2,6},{6,10},{... | collective-permute-start | bytes 786440 | tf_op jit(solution)/shard_map/ppermute | solution.py:95
  96.0 1.9 copy-start.2
  97.8 92.5 %reduce-scatter.2.cloned.1.call-start = ((), (), s32[]{:S(2)}) async-start(), calls=%async_computation.3 | async-start | bytes 1310720 | tf_op jit(solution)/shard_map/reduce_scatter | solution.py:136
  97.9 53.2 %copy-start.9 = (f32[1024]{0:T(1024)S(1)}, f32[1024]{0:T(1024)}, u32[]{:S(2)}) copy-start(f32[1024]{0:T(1024)} %param.22) | copy-start | bytes 12292
  148.6 2.4 %copy-start.4 = (bf16[2,1024,256]{2,1,0:T(8,128)(2,1)S(1)}, bf16[2,1024,256]{2,1,0:T(8,128)(2,1)}, u32[]{:S(2)}) copy-start(bf16[2,1024,256]{2,1,0:T(8,128)(2,1)} %param.23) | copy-start | bytes 3145732
  151.6 7.8 %copy-start.7 = (bf16[256,1024]{1,0:T(8,128)(2,1)S(1)}, bf16[256,1024]{1,0:T(8,128)(2,1)}, u32[]{:S(2)}) copy-start(bf16[256,1024]{1,0:T(8,128)(2,1)} %param.27) | copy-start | bytes 1572868
  151.6 7.8 %copy-start.10 = (f32[256]{0:T(256)S(1)}, f32[256]{0:T(256)}, u32[]{:S(2)}) copy-start(f32[256]{0:T(256)} %param.26) | copy-start | bytes 3076
  151.6 7.8 %copy-start.11 = (f32[256]{0:T(256)S(1)}, f32[256]{0:T(256)}, u32[]{:S(2)}) copy-start(f32[256]{0:T(256)} %param.25) | copy-start | bytes 3076
  152.2 5.9 %collective-permute-start.4 = (bf16[15,256]{1,0:T(8,128)(2,1)S(1)}, bf16[15,256]{1,0:T(8,128)(2,1)S(1)}, u32[]{:S(2)}, u32[]{:S(2)}) collective-permute-start(bf16[15,256]{1,0:T(8,128)(2,1)S(1)} %get-tuple-element.126), channel_id=1, source_target_pairs={{4,0},{8,4},{12,8},{5,1},{9,5},{13,9},{6,2},{10,6},{14,10},{7,3},{... | collective-permute-start | bytes 23048 | tf_op jit(solution)/shard_map/ppermute | solution.py:19
  153.5 5.9 %collective-permute-start.3 = (bf16[15,256]{1,0:T(8,128)(2,1)S(1)}, bf16[15,256]{1,0:T(8,128)(2,1)S(1)}, u32[]{:S(2)}, u32[]{:S(2)}) collective-permute-start(bf16[15,256]{1,0:T(8,128)(2,1)S(1)} %get-tuple-element.125), channel_id=1, source_target_pairs={{0,4},{4,8},{8,12},{1,5},{5,9},{9,13},{2,6},{6,10},{10,14},{3,7},{... | collective-permute-start | bytes 23048 | tf_op jit(solution)/shard_map/ppermute | solution.py:16
Sparse Core Ops, SparseCore 0:
  14.9 33.2 all-gather.2
  97.9 50.6 all-reduce.1
  164.4 25.8 reduce-scatter.1
